TPU v7x, 32 devices: a whole 2x2x4 slice. The times are simulated.
32 devices in a mesh: groups: 2 (over x), gz: 16 (over z, y, core).
Axes of the slice: x: 2, y: 2, z: 4, core: 2. Of those that a mesh axis runs over, the one named last changes fastest.
Arguments:
- positions: float32 [32, 2, 4096], P(('groups', 'gz')), parts along dimension 0, may hold values from -6 to 6
- edges: int32 [32, 2, 8192], P(('groups', 'gz')), parts along dimension 0, may hold values from 0 to 4095
- rest_length: float32 [32, 8192], P(('groups', 'gz')), parts along dimension 0, may hold values from 0.5 to 2
- stiffness: float32 [32, 8192], P(('groups', 'gz')), parts along dimension 0, may hold values from 0.5 to 18, as said below
- corr_index: int32 [32, 2, 1024], P(('groups', 'gz')), parts along dimension 0, may hold values from 0 to 4095
- corr_count: int32 [32], P(('groups', 'gz')), parts along dimension 0, may hold values from 0 to 1024, as said below
- fixed: int32 [32], P(('groups', 'gz')), parts along dimension 0, may hold values 0 or 1
Outputs:
- solution_field: float32 [32, 2, 4096], P(('groups', 'gz')), parts along dimension 0
- residual: float32 [32, 2, 4096], P(('groups', 'gz')), parts along dimension 0
There are 2 independent parts, one for each index of `groups`. A program takes and returns all parts, laid end to end along the dimension named above; each array names one. Nothing has to cross between parts.
Inputs may be any that keep to these rules, and one draw needn't show every extreme that they name: `stiffness`: sections further down the slab tend to be stiffer. `corr_count`: the last pair has count 0; in every draw one pair has exactly 1024 live slots. `corr_index`: slots at or past a pair's count carry no correspondence.
All inputs are finite; a program needn't handle non-finite values. No bound on the sum of `fixed` on one device may be relied on, other than what follows from the above.
Results may differ from a plain program's by a relative error of at most 0.00015.
Values sent between devices are 32-bit elements; how exact they have to be, the bound alone decides.
A program may use at most 64 MiB of HBM per device.

v0:
```python
import jax
import jax.numpy as jnp
from jax import lax
from jax.sharding import PartitionSpec as P

ITERS = 4


DAMPING = 0.05


def shifted(value, axis, steps):
    count = lax.axis_size(axis)
    first, last = (max(0, -steps), min(count, count - steps))
    return lax.ppermute(value, axis, [(source, source + steps) for source in range(first, last)])


def shards(positions, edges, rest_length, stiffness, corr_index, corr_count, fixed):
    points = positions[0]
    head_idx = edges[0, 0]
    tail_idx = edges[0, 1]
    near_idx = corr_index[0, 0]
    far_idx = corr_index[0, 1]
    slots = lax.iota(jnp.int32, near_idx.shape[0])
    active = (slots < corr_count[0]).astype(jnp.float32)[None, :]
    movable = (1 - fixed[0]).astype(jnp.float32)
    spread = points[:, head_idx] - points[:, tail_idx]
    length = jnp.sqrt(jnp.sum(spread * spread, axis=0) + 1.0)
    spring_res = stiffness[0] * (length - rest_length[0])
    slopes = stiffness[0] * spread / length

    def fetch(field):
        next_field = shifted(field, "gz", -1)
        return next_field[:, far_idx]

    def deliver(accum, values):
        returned = jnp.zeros_like(accum).at[:, far_idx].add(-values)
        return accum + shifted(returned, "gz", 1)

    def adjoint(spring_part, corr_part):
        terms = slopes * spring_part[None, :]
        accum = jnp.zeros_like(points).at[:, head_idx].add(terms)
        accum = accum.at[:, tail_idx].add(-terms)
        values = active * corr_part
        accum = accum.at[:, near_idx].add(values)
        return deliver(accum, values)

    corr_res = active * (points[:, near_idx] - fetch(points))
    gradient = -movable * adjoint(spring_res, corr_res)
    solution = jnp.zeros_like(points)
    residual = gradient

    def total_squares(vector):
        return lax.psum(jnp.sum(vector * vector), "gz")

    search = gradient
    norm_now = total_squares(residual)
    for turn in range(ITERS):
        forward_field = movable * search
        forward_spring_part = jnp.sum(
            slopes * (forward_field[:, head_idx] - forward_field[:, tail_idx]), axis=0
        )
        forward_corr_part = active * (forward_field[:, near_idx] - fetch(forward_field))
        image = movable * adjoint(forward_spring_part, forward_corr_part) + DAMPING * search
        step_size = norm_now / lax.psum(jnp.sum(search * image), "gz")
        solution = solution + step_size * search
        residual = residual - step_size * image
        norm_next = total_squares(residual)
        search = residual + norm_next / norm_now * search
        norm_now = norm_next
    return (solution[None], residual[None])


def solution(mesh):
    return jax.shard_map(
        shards,
        mesh=mesh,
        in_specs=(
            P(("groups", "gz"), None, None),
            P(("groups", "gz"), None, None),
            P(("groups", "gz"), None),
            P(("groups", "gz"), None),
            P(("groups", "gz"), None, None),
            P(("groups", "gz")),
            P(("groups", "gz")),
        ),
        out_specs=(P(("groups", "gz"), None, None), P(("groups", "gz"), None, None)),
        check_vma=False,
    )
```

profile of v0, /device:TPU:0, one launch (start us, length us, event | category | flops | bytes accessed | tf_op | source)
XLA Modules:
  0.0 1181.3 jit_solution(9161246351147141710)
XLA Ops:
  4.1 27.7 %gather_fusion.2 = f32[8192,2]{1,0:T(8,128)} fusion(f32[2,4096]{0,1:T(8,128)S(1)} %bitcast.24, s32[8192]{0:T(1024)S(1)} %broadcast_clamp_fusion.1), kind=kCustom, calls=%fused_computation.2 | custom fusion | bytes 163840 | tf_op jit(solution)/shard_map/gather | solution.py:27
  31.8 27.7 %gather_fusion.3 = f32[8192,2]{1,0:T(8,128)} fusion(f32[2,4096]{0,1:T(8,128)S(1)} %bitcast.25, s32[8192]{0:T(1024)S(1)} %broadcast_clamp_fusion), kind=kCustom, calls=%fused_computation.3 | custom fusion | bytes 163840 | tf_op jit(solution)/shard_map/gather | solution.py:27
  59.6 4.8 multiply_reduce_fusion.4
  65.5 5.8 multiply_divide_fusion
  77.6 7.1 scatter_custom_fusion
  85.2 3.0 collective-permute-start.1
  89.8 49.3 %scatter_custom_fusion.1 = f32[2,4096]{0,1:T(8,128)S(1)} fusion(f32[2,4096]{0,1:T(8,128)S(1)} %copy.42, s32[8192]{0:T(1024)S(1)} %bitcast.38, f32[8192,2]{1,0:T(8,128)} %multiply_divide_fusion, f32[8192]{0:T(1024)S(1)} %bitcast.27), kind=kCustom, calls=%fused_computation.68 | custom fusion | flops 32768 | bytes 131072 | tf_op jit(solution)/shard_map/scatter-add | solution.py:42
  139.1 49.4 %scatter_custom_fusion.2 = f32[2,4096]{0,1:T(8,128)S(1)} fusion(f32[2,4096]{0,1:T(8,128)S(1)} %scatter_custom_fusion.1, s32[8192]{0:T(1024)S(1)} %bitcast.32, f32[8192,2]{1,0:T(8,128)} %multiply_divide_fusion, f32[8192]{0:T(1024)S(1)} %bitcast.28), kind=kCustom, calls=%fused_computation.48 | custom fusion | flops 49152 | bytes 131072 | tf_op jit(solution)/shard_map/scatter-add | solution.py:43
  188.5 7.0 scatter_custom_fusion.3
  198.1 27.7 %gather_fusion.6 = f32[8192,2]{1,0:T(8,128)} fusion(f32[2,4096]{0,1:T(8,128)S(1)} %copy.44, s32[8192]{0:T(1024)S(1)} %broadcast_clamp_fusion.1), kind=kCustom, calls=%fused_computation.6 | custom fusion | bytes 163840 | tf_op jit(solution)/shard_map/gather | solution.py:61
  225.8 27.7 %gather_fusion.7 = f32[8192,2]{1,0:T(8,128)} fusion(f32[2,4096]{0,1:T(8,128)S(1)} %copy.44, s32[8192]{0:T(1024)S(1)} %broadcast_clamp_fusion), kind=kCustom, calls=%fused_computation.7 | custom fusion | bytes 163840 | tf_op jit(solution)/shard_map/gather | solution.py:61
  259.8 7.1 scatter_custom_fusion.4
  267.5 5.3 collective-permute-start.3
  272.8 5.8 multiply_reduce_fusion.3
  279.3 49.3 %scatter_custom_fusion.5 = f32[2,4096]{0,1:T(8,128)S(1)} fusion(f32[2,4096]{0,1:T(8,128)S(1)} %copy.49, s32[8192]{0:T(1024)S(1)} %bitcast.39, f32[8192,2]{1,0:T(8,128)} %multiply_divide_fusion, f32[8192]{0:T(1024)S(1)} %multiply_reduce_fusion.3), kind=kCustom, calls=%fused_computation.65 | custom fusion | flops 32768 | bytes 131072 | tf_op jit(solution)/shard_map/scatter-add | solution.py:42
  328.6 49.8 %scatter_custom_fusion.6 = f32[2,4096]{0,1:T(8,128)S(1)} fusion(f32[2,4096]{0,1:T(8,128)S(1)} %scatter_custom_fusion.5, s32[8192]{0:T(1024)S(1)} %bitcast.33, f32[8192,2]{1,0:T(8,128)} %multiply_divide_fusion, f32[8192]{0:T(1024)S(1)} %multiply_reduce_fusion.3), kind=kCustom, calls=%fused_computation.46 | custom fusion | flops 49152 | bytes 131072 | tf_op jit(solution)/shard_map/scatter-add | solution.py:43
  378.4 6.8 scatter_custom_fusion.7
  386.5 34.8 %all-reduce = (f32[]{:T(128)}, f32[]{:T(128)}) all-reduce(f32[]{:T(128)} %get-tuple-element.9, f32[]{:T(128)} %get-tuple-element.8), channel_id=1, replica_groups=mesh['groups'=2,'gz'=16] {'gz'}, use_global_device_ids=true, to_apply=%region_6.0 | all-reduce | flops 2 | bytes 16 | tf_op jit(solution)/shard_map/psum | solution.py:54
  423.3 30.1 %psum.58 = f32[]{:T(128)} all-reduce(f32[]{:T(128)} %get-tuple-element.20), channel_id=1, replica_groups=mesh['groups'=2,'gz'=16] {'gz'}, use_global_device_ids=true, to_apply=%region_15.0 | all-reduce | flops 1 | bytes 8 | tf_op jit(solution)/shard_map/psum | solution.py:54
  456.7 27.7 %gather_fusion.10 = f32[8192,2]{1,0:T(8,128)} fusion(f32[2,4096]{0,1:T(8,128)S(1)} %copy.51, s32[8192]{0:T(1024)S(1)} %broadcast_clamp_fusion.1), kind=kCustom, calls=%fused_computation.10 | custom fusion | bytes 163840 | tf_op jit(solution)/shard_map/gather | solution.py:61
  484.4 27.7 %gather_fusion.11 = f32[8192,2]{1,0:T(8,128)} fusion(f32[2,4096]{0,1:T(8,128)S(1)} %copy.51, s32[8192]{0:T(1024)S(1)} %broadcast_clamp_fusion), kind=kCustom, calls=%fused_computation.11 | custom fusion | bytes 163840 | tf_op jit(solution)/shard_map/gather | solution.py:61
  518.4 7.1 scatter_custom_fusion.8
  526.1 3.0 collective-permute-start.5
  529.2 5.8 multiply_reduce_fusion.2
  535.7 49.5 %scatter_custom_fusion.9 = f32[2,4096]{0,1:T(8,128)S(1)} fusion(f32[2,4096]{0,1:T(8,128)S(1)} %copy.56, s32[8192]{0:T(1024)S(1)} %bitcast.40, f32[8192,2]{1,0:T(8,128)} %multiply_divide_fusion, f32[8192]{0:T(1024)S(1)} %multiply_reduce_fusion.2), kind=kCustom, calls=%fused_computation.62 | custom fusion | flops 32768 | bytes 131072 | tf_op jit(solution)/shard_map/scatter-add | solution.py:42
  585.2 49.4 %scatter_custom_fusion.10 = f32[2,4096]{0,1:T(8,128)S(1)} fusion(f32[2,4096]{0,1:T(8,128)S(1)} %scatter_custom_fusion.9, s32[8192]{0:T(1024)S(1)} %bitcast.34, f32[8192,2]{1,0:T(8,128)} %multiply_divide_fusion, f32[8192]{0:T(1024)S(1)} %multiply_reduce_fusion.2), kind=kCustom, calls=%fused_computation.44 | custom fusion | flops 49152 | bytes 131072 | tf_op jit(solution)/shard_map/scatter-add | solution.py:43
  634.5 6.8 scatter_custom_fusion.11
  642.6 31.2 %psum.59 = f32[]{:T(128)} all-reduce(f32[]{:T(128)} %multiply_reduce_fusion.9), channel_id=1, replica_groups=mesh['groups'=2,'gz'=16] {'gz'}, use_global_device_ids=true, to_apply=%region_22.0 | all-reduce | flops 1 | bytes 8 | tf_op jit(solution)/shard_map/psum | solution.py:65
  675.7 30.1 %psum.60 = f32[]{:T(128)} all-reduce(f32[]{:T(128)} %get-tuple-element.16), channel_id=1, replica_groups=mesh['groups'=2,'gz'=16] {'gz'}, use_global_device_ids=true, to_apply=%region_24.0 | all-reduce | flops 1 | bytes 8 | tf_op jit(solution)/shard_map/psum | solution.py:54
  709.2 27.7 %gather_fusion.14 = f32[8192,2]{1,0:T(8,128)} fusion(f32[2,4096]{0,1:T(8,128)S(1)} %copy.58, s32[8192]{0:T(1024)S(1)} %broadcast_clamp_fusion.1), kind=kCustom, calls=%fused_computation.14 | custom fusion | bytes 163840 | tf_op jit(solution)/shard_map/gather | solution.py:61
  736.9 27.7 %gather_fusion.15 = f32[8192,2]{1,0:T(8,128)} fusion(f32[2,4096]{0,1:T(8,128)S(1)} %copy.58, s32[8192]{0:T(1024)S(1)} %broadcast_clamp_fusion), kind=kCustom, calls=%fused_computation.15 | custom fusion | bytes 163840 | tf_op jit(solution)/shard_map/gather | solution.py:61
  770.9 7.1 scatter_custom_fusion.12
  778.6 3.2 collective-permute-start.7
  781.9 5.8 multiply_reduce_fusion.1
  788.3 49.3 %scatter_custom_fusion.13 = f32[2,4096]{0,1:T(8,128)S(1)} fusion(f32[2,4096]{0,1:T(8,128)S(1)} %copy.63, s32[8192]{0:T(1024)S(1)} %bitcast.41, f32[8192,2]{1,0:T(8,128)} %multiply_divide_fusion, f32[8192]{0:T(1024)S(1)} %multiply_reduce_fusion.1), kind=kCustom, calls=%fused_computation.59 | custom fusion | flops 32768 | bytes 131072 | tf_op jit(solution)/shard_map/scatter-add | solution.py:42
  837.7 49.4 %scatter_custom_fusion.14 = f32[2,4096]{0,1:T(8,128)S(1)} fusion(f32[2,4096]{0,1:T(8,128)S(1)} %scatter_custom_fusion.13, s32[8192]{0:T(1024)S(1)} %bitcast.35, f32[8192,2]{1,0:T(8,128)} %multiply_divide_fusion, f32[8192]{0:T(1024)S(1)} %multiply_reduce_fusion.1), kind=kCustom, calls=%fused_computation.42 | custom fusion | flops 49152 | bytes 131072 | tf_op jit(solution)/shard_map/scatter-add | solution.py:43
  887.0 6.8 scatter_custom_fusion.15
  895.1 31.2 %psum.61 = f32[]{:T(128)} all-reduce(f32[]{:T(128)} %multiply_reduce_fusion.7), channel_id=1, replica_groups=mesh['groups'=2,'gz'=16] {'gz'}, use_global_device_ids=true, to_apply=%region_31.0 | all-reduce | flops 1 | bytes 8 | tf_op jit(solution)/shard_map/psum | solution.py:65
  928.3 30.1 %psum.62 = f32[]{:T(128)} all-reduce(f32[]{:T(128)} %get-tuple-element.12), channel_id=1, replica_groups=mesh['groups'=2,'gz'=16] {'gz'}, use_global_device_ids=true, to_apply=%region_33.0 | all-reduce | flops 1 | bytes 8 | tf_op jit(solution)/shard_map/psum | solution.py:54
  961.9 27.7 %gather_fusion.18 = f32[8192,2]{1,0:T(8,128)} fusion(f32[2,4096]{0,1:T(8,128)S(1)} %copy.65, s32[8192]{0:T(1024)S(1)} %broadcast_clamp_fusion.1), kind=kCustom, calls=%fused_computation.18 | custom fusion | bytes 163840 | tf_op jit(solution)/shard_map/gather | solution.py:61
  989.7 27.7 %gather_fusion.19 = f32[8192,2]{1,0:T(8,128)} fusion(f32[2,4096]{0,1:T(8,128)S(1)} %copy.65, s32[8192]{0:T(1024)S(1)} %broadcast_clamp_fusion), kind=kCustom, calls=%fused_computation.19 | custom fusion | bytes 163840 | tf_op jit(solution)/shard_map/gather | solution.py:61
  1023.7 7.1 scatter_custom_fusion.16
  1031.4 3.0 collective-permute-start.9
  1034.4 5.8 multiply_reduce_fusion
  1040.9 49.3 %scatter_custom_fusion.17 = f32[2,4096]{0,1:T(8,128)S(1)} fusion(f32[2,4096]{0,1:T(8,128)S(1)} %copy.70, s32[8192]{0:T(1024)S(1)} %bitcast.42, f32[8192,2]{1,0:T(8,128)} %multiply_divide_fusion, f32[8192]{0:T(1024)S(1)} %multiply_reduce_fusion), kind=kCustom, calls=%fused_computation.56 | custom fusion | flops 32768 | bytes 131072 | tf_op jit(solution)/shard_map/scatter-add | solution.py:42
  1090.2 49.4 %scatter_custom_fusion.18 = f32[2,4096]{0,1:T(8,128)S(1)} fusion(f32[2,4096]{0,1:T(8,128)S(1)} %scatter_custom_fusion.17, s32[8192]{0:T(1024)S(1)} %bitcast.36, f32[8192,2]{1,0:T(8,128)} %multiply_divide_fusion, f32[8192]{0:T(1024)S(1)} %multiply_reduce_fusion), kind=kCustom, calls=%fused_computation.40 | custom fusion | flops 49152 | bytes 131072 | tf_op jit(solution)/shard_map/scatter-add | solution.py:43
  1139.6 6.8 scatter_custom_fusion.19
  1147.6 31.2 %psum.63 = f32[]{:T(128)} all-reduce(f32[]{:T(128)} %multiply_reduce_fusion.5), channel_id=1, replica_groups=mesh['groups'=2,'gz'=16] {'gz'}, use_global_device_ids=true, to_apply=%region_40.0 | all-reduce | flops 1 | bytes 8 | tf_op jit(solution)/shard_map/psum | solution.py:65
  (84 shorter events, 58.0 us)
Async XLA Ops:
  0.6 3.4 copy-start.3
  2.7 71.4 %collective-permute-start = (f32[2,4096]{1,0:T(2,128)S(1)}, f32[2,4096]{1,0:T(2,128)S(1)}, u32[]{:S(2)}, u32[]{:S(2)}) collective-permute-start(f32[2,4096]{1,0:T(2,128)S(1)} %copy.39), channel_id=1, source_target_pairs={{1,0},{2,1},{3,2},{4,3},{5,4},{6,5},{7,6},{8,7},{9,8},{10,9},{11,1... | collective-permute-start | bytes 98312 | tf_op jit(solution)/shard_map/ppermute | solution.py:15
  59.5 4.8 copy-start.5
  59.5 5.6 copy-start
  59.5 5.9 copy-start.1
  59.5 5.9 copy-start.2
  77.5 10.7 copy-start.4
  85.2 3.9 collective-permute-start.1
  196.1 60.2 %collective-permute-start.2 = (f32[2,4096]{1,0:T(2,128)S(1)}, f32[2,4096]{1,0:T(2,128)S(1)}, u32[]{:S(2)}, u32[]{:S(2)}) collective-permute-start(f32[2,4096]{1,0:T(2,128)S(1)} %broadcast_multiply_fusion.3), channel_id=1, source_target_pairs={{1,0},{2,1},{3,2},{4,3},{5,4},{6,5},{7,6},{8,7},{9,8},{10,9},{11,1... | collective-permute-start | bytes 98312 | tf_op jit(solution)/shard_map/ppermute | solution.py:15
  267.5 11.1 collective-permute-start.3
  454.7 60.2 %collective-permute-start.4 = (f32[2,4096]{1,0:T(2,128)S(1)}, f32[2,4096]{1,0:T(2,128)S(1)}, u32[]{:S(2)}, u32[]{:S(2)}) collective-permute-start(f32[2,4096]{1,0:T(2,128)S(1)} %get-tuple-element.18), channel_id=1, source_target_pairs={{1,0},{2,1},{3,2},{4,3},{5,4},{6,5},{7,6},{8,7},{9,8},{10,9},{11,1... | collective-permute-start | bytes 98312 | tf_op jit(solution)/shard_map/ppermute | solution.py:15
  526.1 8.9 collective-permute-start.5
  707.2 60.2 %collective-permute-start.6 = (f32[2,4096]{1,0:T(2,128)S(1)}, f32[2,4096]{1,0:T(2,128)S(1)}, u32[]{:S(2)}, u32[]{:S(2)}) collective-permute-start(f32[2,4096]{1,0:T(2,128)S(1)} %get-tuple-element.14), channel_id=1, source_target_pairs={{1,0},{2,1},{3,2},{4,3},{5,4},{6,5},{7,6},{8,7},{9,8},{10,9},{11,1... | collective-permute-start | bytes 98312 | tf_op jit(solution)/shard_map/ppermute | solution.py:15
  778.6 9.1 collective-permute-start.7
  959.7 60.5 %collective-permute-start.8 = (f32[2,4096]{1,0:T(2,128)S(1)}, f32[2,4096]{1,0:T(2,128)S(1)}, u32[]{:S(2)}, u32[]{:S(2)}) collective-permute-start(f32[2,4096]{1,0:T(2,128)S(1)} %broadcast_multiply_fusion), channel_id=1, source_target_pairs={{1,0},{2,1},{3,2},{4,3},{5,4},{6,5},{7,6},{8,7},{9,8},{10,9},{11,1... | collective-permute-start | bytes 98312 | tf_op jit(solution)/shard_map/ppermute | solution.py:15
  1031.4 8.9 collective-permute-start.9
where the time goes:
time: 1190 us; the launch traced here: 1180 us
  other arithmetic  603 us (51%)
  local copies, waits for them, and re-layouts  323 us (27%)
  blocking collectives  219 us (18%)
  starting transfers between devices  24.3 us (2%)
  between operations  12.5 us (1%)
    scatter-add x5, other arithmetic, adjoint(): accum = accum.at[:, tail_idx].add(-terms)  247 us
    scatter-add x5, other arithmetic, adjoint(): accum = jnp.zeros_like(points).at[:, head_idx].add(terms)  247 us
    psum x4, blocking collectives, total_squares(): return lax.psum(jnp.sum(vector * vector), 'gz')  125 us
    gather x4, local copies, waits for them, and re-layouts, shards(): forward_field[:, head_idx] - forward_field[:, tail_idx]  111 us
    gather x4, local copies, waits for them, and re-layouts, shards(): forward_field[:, tail_idx]  111 us
    psum x3, blocking collectives, shards(): step_size = norm_now / lax.psum(jnp.sum(search * image), 'gz')  93.6 us
    gather x2, local copies, waits for them, and re-layouts, shards(): spread = points[:, head_idx] - points[:, tail_idx]  55.4 us
    scatter-add x5, other arithmetic, deliver(): returned = jnp.zeros_like(accum).at[:, far_idx].add(-values)  35.3 us
  transfers between devices with their start and end apart: 10, of which 1 were waited for; matrix products, arithmetic and copies ran while one was open for 28% of the time, Pallas kernels for 0%

commit v1 on v0

v1 whole, which is shorter than its diff:
```python
import functools

import jax
import jax.numpy as jnp
from jax import lax
from jax.experimental import pallas as pl
from jax.experimental.pallas import tpu as pltpu
from jax.sharding import PartitionSpec as P

ITERS = 4
DAMPING = 0.05
LANES = 128
GROUP = 8
MESH = pl.DeviceIdType.MESH


def pick(line_of, parts, blocks):
    outs = [[jnp.zeros(lo.shape, jnp.float32) for _ in range(2)] for lo, _ in blocks]
    for h in range(parts):
        for c in range(2):
            line = line_of(c * parts + h)
            for k, (lo, hi) in enumerate(blocks):
                got = jnp.take_along_axis(
                    jnp.broadcast_to(line, lo.shape), lo, axis=1, mode="promise_in_bounds"
                )
                outs[k][c] = jnp.where(hi == h, got, outs[k][c])
    return outs


def split_index(index):
    return index & (LANES - 1), index >> 7


def kernel(
    count,
    corr_count, fixed, positions, edges, rest_length, stiffness, corr_index,
    solution_out, residual_out,
    index, rest, stiff, lo_hot, hi_hot, slope, spring, spring_old, corr_old, terms,
    table, next_table, far_here, far_prev, corr_send, corr_recv, sums, search,
    table_sems, corr_sems, sum_sems, far_sems,
):
    me = lax.axis_index("gz")
    has_next = me < count - 1
    has_prev = me > 0
    upper = {"gz": jnp.minimum(me + 1, count - 1)}
    lower = {"gz": jnp.maximum(me - 1, 0)}
    parts = positions.shape[2] // LANES
    springs = rest_length.shape[1] // LANES
    slots = corr_index.shape[2] // LANES
    groups = springs // GROUP
    wide = GROUP * LANES
    f32, bf16 = jnp.float32, jnp.bfloat16

    barrier = pltpu.get_barrier_semaphore()
    for step in range(1, count):
        other = lax.rem(me + step, count)
        pl.semaphore_signal(barrier, inc=1, device_id={"gz": other}, device_id_type=MESH)

    def lanes(k):
        return slice(k * LANES, (k + 1) * LANES)

    for s in range(slots):
        far_here[s : s + 1, :] = corr_index[0, 1:2, lanes(s)]
        index[2 * springs + s : 2 * springs + s + 1, :] = corr_index[0, 0:1, lanes(s)]
    for c in range(2):
        for h in range(parts):
            table[0, c * parts + h : c * parts + h + 1, :] = positions[0, c : c + 1, lanes(h)]
    for k in range(springs):
        index[k : k + 1, :] = edges[0, 0:1, lanes(k)]
        index[springs + k : springs + k + 1, :] = edges[0, 1:2, lanes(k)]
        rest[k : k + 1, :] = rest_length[0:1, lanes(k)]
        stiff[k : k + 1, :] = stiffness[0:1, lanes(k)]

    @pl.when(me == 0)
    def _():
        far_prev[...] = jnp.zeros_like(far_prev)
        corr_recv[...] = jnp.zeros_like(corr_recv)

    @pl.when(me == count - 1)
    def _():
        next_table[...] = jnp.zeros_like(next_table)

    search[...] = jnp.zeros_like(search)
    spring_old[...] = jnp.zeros_like(spring_old)
    corr_old[...] = jnp.zeros_like(corr_old)

    movable = (1 - fixed[0]).astype(f32)
    slot = (
        lax.broadcasted_iota(jnp.int32, (slots, LANES), 0) * LANES
        + lax.broadcasted_iota(jnp.int32, (slots, LANES), 1)
    )
    active = slot < corr_count[0]

    def table_copy(turn):
        return pltpu.make_async_remote_copy(
            src_ref=table.at[turn], dst_ref=next_table.at[turn],
            send_sem=table_sems.at[0, turn], recv_sem=table_sems.at[1, turn],
            device_id=lower, device_id_type=MESH,
        )

    def corr_copy(turn):
        return pltpu.make_async_remote_copy(
            src_ref=corr_send.at[turn], dst_ref=corr_recv.at[turn],
            send_sem=corr_sems.at[0, turn], recv_sem=corr_sems.at[1, turn],
            device_id=upper, device_id_type=MESH,
        )

    far_copy = pltpu.make_async_remote_copy(
        src_ref=far_here, dst_ref=far_prev,
        send_sem=far_sems.at[0], recv_sem=far_sems.at[1],
        device_id=upper, device_id_type=MESH,
    )

    def sum_start(place, value):
        sums[place, me] = jnp.sum(value, axis=0, keepdims=True)
        for step in range(1, count):
            pltpu.make_async_remote_copy(
                src_ref=sums.at[place, me], dst_ref=sums.at[place, me],
                send_sem=sum_sems.at[0, place], recv_sem=sum_sems.at[1, place],
                device_id={"gz": lax.rem(me + step, count)}, device_id_type=MESH,
            ).start()

    def sum_all(place):
        part = sums.at[place, pl.ds(0, count - 1)]
        return pltpu.make_async_remote_copy(
            src_ref=part, dst_ref=part,
            send_sem=sum_sems.at[0, place], recv_sem=sum_sems.at[1, place],
            device_id={"gz": lax.rem(me + 1, count)}, device_id_type=MESH,
        )

    def sum_finish(place):
        sum_all(place).wait_recv()
        return jnp.sum(jnp.sum(sums[place], axis=0), axis=1, keepdims=True)

    pl.semaphore_wait(barrier, count - 1)

    @pl.when(has_next)
    def _():
        far_copy.start()

    @pl.when(has_prev)
    def _():
        table_copy(0).start()

    def hot(line, chunk, sign):
        lo, hi = split_index(line)
        at = pl.ds(pl.multiple_of(chunk * LANES, LANES), LANES)
        rows = lax.broadcasted_iota(jnp.int32, (LANES, LANES), 0)
        lo_hot[:, at] = jnp.where(lo == rows, 1.0, 0.0).astype(bf16)
        rows = lax.broadcasted_iota(jnp.int32, (parts, LANES), 0)
        hi_hot[:, at] = jnp.where(hi == rows, sign, 0.0).astype(bf16)

    def hot_springs(k, _):
        hot(index[pl.ds(k, 1), :], k, 1.0)
        hot(index[pl.ds(springs + k, 1), :], springs + k, -1.0)
        return 0

    lax.fori_loop(0, springs, hot_springs, 0)
    for s in range(slots):
        hot(index[2 * springs + s : 2 * springs + s + 1, :], 2 * springs + s, 1.0)

    def rows_of(k):
        return pl.ds(pl.multiple_of(k * GROUP, GROUP), GROUP)

    def spread_of(turn, k):
        head = split_index(index[rows_of(k), :])
        tail = split_index(index[rows_of(k + groups), :])
        a, b = pick(lambda row: table[turn, row : row + 1, :], parts, [head, tail])
        return a[0] - b[0], a[1] - b[1]

    def corr_parts(turn):
        near = split_index(index[2 * springs : 2 * springs + slots, :])
        (a,) = pick(lambda row: table[turn, row : row + 1, :], parts, [near])

        @pl.when(has_next)
        def _():
            table_copy(turn).wait_recv()

        far = split_index(far_here[...])
        (b,) = pick(lambda row: next_table[turn, row : row + 1, :], parts, [far])
        return [jnp.where(active, a[c] - b[c], 0.0) for c in range(2)]

    def put_terms(c, rows, value):
        first = value.astype(bf16).astype(f32)
        terms[2 * c, rows, :] = first
        terms[2 * c + 1, rows, :] = value - first

    def spread_terms(row, lines):
        made = [[] for _ in lines]
        for i in range(GROUP):
            pieces = [[] for _ in lines]
            for part in range(4):
                value = jnp.broadcast_to(terms[part, pl.ds(row + i, 1), :], (parts, LANES)).astype(bf16)
                for piece, line in zip(pieces, lines):
                    at = pl.ds(pl.multiple_of((line + i) * LANES, LANES), LANES)
                    piece.append(value * hi_hot[:, at])
            for k, piece in enumerate(pieces):
                made[k].append(jnp.concatenate(piece, axis=0))
        return [jnp.concatenate(m, axis=1) for m in made]

    def add_terms(total, row, lines):
        for left, line in zip(spread_terms(row, lines), lines):
            right = lo_hot[:, pl.ds(pl.multiple_of(line * LANES, LANES), wide)]
            total += lax.dot_general(left, right, (((1,), (1,)), ((), ())), preferred_element_type=f32)
        return total

    def adjoint(turn, ready):
        def body(k, total):
            return add_terms(total, k * GROUP, (k * GROUP, springs + k * GROUP))

        total = lax.fori_loop(0, groups, body, jnp.zeros((4 * parts, LANES), f32))
        for s in range(0, slots, GROUP):
            total = add_terms(total, springs + s, (2 * springs + s,))
        ready()

        @pl.when(has_prev)
        def _():
            corr_copy(turn).wait_recv()

        for c in range(2):
            put_terms(c, pl.ds(springs + slots, slots), corr_recv[turn, c])
        for s in range(0, slots, GROUP):
            total = add_terms(total, springs + slots + s, (2 * springs + slots + s,))
        return jnp.concatenate(
            [total[2 * c * parts : (2 * c + 1) * parts] + total[(2 * c + 1) * parts : (2 * c + 2) * parts]
             for c in range(2)], axis=0,
        )

    def send_corr(turn, value):
        for c in range(2):
            corr_send[turn, c] = value[c]
            put_terms(c, pl.ds(springs, slots), value[c])

        @pl.when(has_next)
        def _():
            corr_copy(turn).start()

    def first_springs(k, _):
        dx, dy = spread_of(0, k)
        rows = rows_of(k)
        length = jnp.sqrt((dx * dx + dy * dy) + 1.0)
        part = stiff[rows, :] * (length - rest[rows, :])
        for c, d in enumerate((dx, dy)):
            value = stiff[rows, :] * d / length
            slope[c, rows, :] = value
            put_terms(c, rows, value * part)
        return 0

    lax.fori_loop(0, groups, first_springs, 0)
    send_corr(0, corr_parts(0))

    def far_ready():
        @pl.when(has_prev)
        def _():
            far_copy.wait_recv()

        for s in range(slots):
            hot(far_prev[s : s + 1, :], 2 * springs + slots + s, -1.0)

    residual_out[...] = -movable * adjoint(0, far_ready)
    solution_out[...] = jnp.zeros_like(solution_out)

    def folded(value):
        return jnp.sum(value.reshape(-1, 8, LANES), axis=0)

    def turn_body(turn, norm_before):
        place = 2 * (turn - 1)
        residual = residual_out[...]
        table[turn] = movable * residual

        @pl.when(has_prev)
        def _():
            table_copy(turn).start()

        sum_start(place, folded(residual * residual))

        def springs_body(k, _):
            dx, dy = spread_of(turn, k)
            rows = rows_of(k)
            spring[rows, :] = slope[0, rows, :] * dx + slope[1, rows, :] * dy
            return 0

        lax.fori_loop(0, groups, springs_body, 0)
        corr = corr_parts(turn)
        norm_now = sum_finish(place)
        ratio = jnp.where(turn == 1, 0.0, norm_now / norm_before)
        corr = [corr[c] + ratio * corr_old[c] for c in range(2)]
        for c in range(2):
            corr_old[c] = corr[c]
        send_corr(turn, corr)
        direction = residual_out[...] + ratio * search[...]
        search[...] = direction
        stretch = spring[...] + ratio * spring_old[...]
        spring_old[...] = stretch
        power = folded(stretch * stretch) + DAMPING * folded(direction * direction)
        power += folded(corr[0] * corr[0] + corr[1] * corr[1])
        sum_start(place + 1, power)
        for c in range(2):
            put_terms(c, pl.ds(0, springs), slope[c] * stretch)
        image = movable * adjoint(turn, lambda: None) + DAMPING * search[...]
        step_size = norm_now / sum_finish(place + 1)
        solution_out[...] += step_size * search[...]
        residual_out[...] -= step_size * image
        return norm_now

    lax.fori_loop(1, ITERS + 1, turn_body, jnp.ones((1, 1), f32))

    @pl.when(has_next)
    def _():
        far_copy.wait_send()
        for turn in range(ITERS + 1):
            corr_copy(turn).wait_send()

    @pl.when(has_prev)
    def _():
        for turn in range(ITERS + 1):
            table_copy(turn).wait_send()

    for place in range(2 * ITERS):
        sum_all(place).wait_send()


def shards(count, positions, edges, rest_length, stiffness, corr_index, corr_count, fixed):
    verts, slots = positions.shape[2] // LANES, corr_index.shape[2] // LANES
    springs = rest_length.shape[1] // LANES
    columns = 2 * (springs + slots) * LANES
    turns = ITERS + 1
    f32 = jnp.float32
    out = jax.ShapeDtypeStruct((2 * verts, LANES), f32)
    vmem, smem = pl.BlockSpec(memory_space=pltpu.VMEM), pl.BlockSpec(memory_space=pltpu.SMEM)
    answer, residual = pl.pallas_call(
        functools.partial(kernel, count),
        out_shape=(out, out),
        in_specs=[smem, smem, vmem, vmem, vmem, vmem, vmem],
        out_specs=(vmem, vmem),
        scratch_shapes=[
            pltpu.VMEM((2 * springs + slots, LANES), jnp.int32),
            pltpu.VMEM((springs, LANES), f32),
            pltpu.VMEM((springs, LANES), f32),
            pltpu.VMEM((LANES, columns), jnp.bfloat16),
            pltpu.VMEM((verts, columns), jnp.bfloat16),
            pltpu.VMEM((2, springs, LANES), f32),
            pltpu.VMEM((springs, LANES), f32),
            pltpu.VMEM((springs, LANES), f32),
            pltpu.VMEM((2, slots, LANES), f32),
            pltpu.VMEM((4, springs + 2 * slots, LANES), f32),
            pltpu.VMEM((turns, 2 * verts, LANES), f32),
            pltpu.VMEM((turns, 2 * verts, LANES), f32),
            pltpu.VMEM((slots, LANES), jnp.int32),
            pltpu.VMEM((slots, LANES), jnp.int32),
            pltpu.VMEM((turns, 2, slots, LANES), f32),
            pltpu.VMEM((turns, 2, slots, LANES), f32),
            pltpu.VMEM((2 * ITERS, count, 1, LANES), f32),
            pltpu.VMEM((2 * verts, LANES), f32),
            pltpu.SemaphoreType.DMA((2, turns)),
            pltpu.SemaphoreType.DMA((2, turns)),
            pltpu.SemaphoreType.DMA((2, 2 * ITERS)),
            pltpu.SemaphoreType.DMA((2,)),
        ],
        compiler_params=pltpu.CompilerParams(
            collective_id=0, has_side_effects=True, vmem_limit_bytes=40 * 2**20
        ),
        name="align",
    )(corr_count, fixed, positions, edges, rest_length, stiffness, corr_index)
    return answer.reshape(positions.shape), residual.reshape(positions.shape)


def solution(mesh):
    row = P(("groups", "gz"))
    return jax.shard_map(
        functools.partial(shards, mesh.shape["gz"]),
        mesh=mesh,
        in_specs=(row,) * 7,
        out_specs=(row, row),
        check_vma=False,
    )
```

time: 1190 us -> 53.3 us (0.04)
  other arithmetic: 603 us -> 0 us
  local copies, waits for them, and re-layouts: 323 us -> 5.07 us
  blocking collectives: 219 us -> 0 us
  Pallas kernels: 0 us -> 45.9 us
  starting transfers between devices: 24.3 us -> 0 us
    scatter-add x20 -> x0, other arithmetic: 563 us -> none  [the longest x5 247 us: adjoint(): accum = accum.at[:, tail_idx].add(-terms)]
    gather x20 -> x0, local copies, waits for them, and re-layouts: 305 us -> none  [the longest x4 111 us: shards(): forward_field[:, head_idx] - forward_field[:, tail_idx]]
    psum x7 -> x0, blocking collectives: 219 us -> none  [the longest x4 125 us: total_squares(): return lax.psum(jnp.sum(vector * vector), 'gz')]
    pallas_call x0 -> x1, Pallas kernels: none -> 45.9 us  [shards(): pl.pallas_call(functools.partial(kernel, count), out_shape=(out, out), in...]
    reduce_sum x12 -> x0, other arithmetic: 32.6 us -> none  [the longest x4 23.3 us: shards(): jnp.sum(slopes * (forward_field[:, head_idx] - forward_field[:, tail_idx]...]
    ppermute x10 -> x0, starting transfers between devices: 24.3 us -> none  [shifted(): lax.ppermute(value, axis, [(source, source + steps) for source in range(f...]
  transfers between devices with their start and end apart: 10 -> 0, of which waited for: 1 -> 0; matrix products, arithmetic and copies ran while one was open for 28% -> 0% of each run, Pallas kernels for 0% -> 0%
where the time goes in v1:
time: 53.3 us; the launch traced here: 52.9 us
  Pallas kernels  45.9 us (86%)
  local copies, waits for them, and re-layouts  5.07 us (10%)
  between operations  1.94 us (4%)
    pallas_call x1, Pallas kernels, shards(): pl.pallas_call(functools.partial(kernel, count), out_shape=(out, out), in...  45.9 us
    unnamed x10, local copies, waits for them, and re-layouts  3.8 us
    reshape x2, local copies, waits for them, and re-layouts, shards(): return (answer.reshape(positions.shape), residual.reshape(positions.shape))  1.27 us

profile of v1, /device:TPU:0, one launch (start us, length us, event | category | flops | bytes accessed | tf_op | source)
XLA Modules:
  0.0 52.9 jit_solution(5775167957246838046)
XLA Ops:
  1.9 0.0 copy-start
  1.9 0.8 %copy-done = s32[1,2,8192]{2,1,0:T(2,128)S(1)} copy-done((s32[1,2,8192]{2,1,0:T(2,128)S(1)}, s32[1,2,8192]{2,1,0:T(2,128)}, u32[]{:S(2)}) %copy-start) | copy-done | bytes 65560
  2.8 0.0 copy-start.1
  2.8 0.8 %copy-done.1 = f32[1,2,4096]{2,1,0:T(2,128)S(1)} copy-done((f32[1,2,4096]{2,1,0:T(2,128)S(1)}, f32[1,2,4096]{2,1,0:T(2,128)}, u32[]{:S(2)}) %copy-start.1) | copy-done | bytes 32792
  3.5 0.0 copy-start.2
  3.5 0.8 %copy-done.2 = f32[1,8192]{1,0:T(1,128)S(1)} copy-done((f32[1,8192]{1,0:T(1,128)S(1)}, f32[1,8192]{1,0:T(1,128)}, u32[]{:S(2)}) %copy-start.2) | copy-done | bytes 32792
  4.3 0.0 copy-start.3
  4.3 0.8 %copy-done.3 = f32[1,8192]{1,0:T(1,128)S(1)} copy-done((f32[1,8192]{1,0:T(1,128)S(1)}, f32[1,8192]{1,0:T(1,128)}, u32[]{:S(2)}) %copy-start.3) | copy-done | bytes 32792
  5.0 0.0 copy-start.4
  5.0 0.7 %copy-done.4 = s32[1,2,1024]{2,1,0:T(2,128)S(1)} copy-done((s32[1,2,1024]{2,1,0:T(2,128)S(1)}, s32[1,2,1024]{2,1,0:T(2,128)}, u32[]{:S(2)}) %copy-start.4) | copy-done | bytes 8216
  5.7 45.9 %align.1 = (f32[64,128]{1,0:T(8,128)S(1)}, f32[64,128]{1,0:T(8,128)S(1)}) custom-call(s32[1]{0:T(128)S(6)} %copy.9.corr_count, s32[1]{0:T(128)S(6)} %copy.10.fixed, f32[1,2,4096]{2,1,0:T(2,128)S(1)} %copy-done.1, s32[1,2,8192]{2,1,0:T(2,128)S(1)} %copy-done, f32[1,8192]{1,0:T(1,128)S(1)} %copy-done.2, f32[1,8192]{1,0:T(1,128)S(1)} %copy-done.3, ...), custom_call_target="tpu_custom_call" | custom-call | tf_op jit(solution)/shard_map/align/pallas_call | solution.py:331
  51.6 0.6 %reshape.10 = f32[1,2,4096]{2,1,0:T(2,128)} reshape(f32[64,128]{1,0:T(8,128)S(1)} %get-tuple-element.4) | data formatting | bytes 65536 | tf_op jit(solution)/shard_map/reshape | solution.py:365
  52.3 0.6 %reshape.11 = f32[1,2,4096]{2,1,0:T(2,128)} reshape(f32[64,128]{1,0:T(8,128)S(1)} %get-tuple-element.5) | data formatting | bytes 65536 | tf_op jit(solution)/shard_map/reshape | solution.py:365
Async XLA Ops:
  1.9 0.8 %copy-start = (s32[1,2,8192]{2,1,0:T(2,128)S(1)}, s32[1,2,8192]{2,1,0:T(2,128)}, u32[]{:S(2)}) copy-start(s32[1,2,8192]{2,1,0:T(2,128)} %edges.1) | copy-start | bytes 196612
  2.8 0.8 %copy-start.1 = (f32[1,2,4096]{2,1,0:T(2,128)S(1)}, f32[1,2,4096]{2,1,0:T(2,128)}, u32[]{:S(2)}) copy-start(f32[1,2,4096]{2,1,0:T(2,128)} %positions.1) | copy-start | bytes 98308
  3.5 0.8 %copy-start.2 = (f32[1,8192]{1,0:T(1,128)S(1)}, f32[1,8192]{1,0:T(1,128)}, u32[]{:S(2)}) copy-start(f32[1,8192]{1,0:T(1,128)} %rest_length.1) | copy-start | bytes 98308
  4.3 0.8 %copy-start.3 = (f32[1,8192]{1,0:T(1,128)S(1)}, f32[1,8192]{1,0:T(1,128)}, u32[]{:S(2)}) copy-start(f32[1,8192]{1,0:T(1,128)} %stiffness.1) | copy-start | bytes 98308
  5.0 0.7 %copy-start.4 = (s32[1,2,1024]{2,1,0:T(2,128)S(1)}, s32[1,2,1024]{2,1,0:T(2,128)}, u32[]{:S(2)}) copy-start(s32[1,2,1024]{2,1,0:T(2,128)} %corr_index.1) | copy-start | bytes 24580

commit v2 on v1

v2 whole, which is shorter than its diff:
```python
import functools

import jax
import jax.numpy as jnp
from jax import lax
from jax.experimental import pallas as pl
from jax.experimental.pallas import tpu as pltpu
from jax.sharding import PartitionSpec as P

ITERS = 4
DAMPING = 0.05
LANES = 128
GROUP = 8
GATHER_UNROLL = 8
SCATTER_UNROLL = 8
MESH = pl.DeviceIdType.MESH


def pick(line_of, parts, blocks):
    outs = [[jnp.zeros(lo.shape, jnp.float32) for _ in range(2)] for lo, _ in blocks]
    for h in range(parts):
        for c in range(2):
            line = line_of(c * parts + h)
            for k, (lo, hi) in enumerate(blocks):
                got = jnp.take_along_axis(
                    jnp.broadcast_to(line, lo.shape), lo, axis=1, mode="promise_in_bounds"
                )
                outs[k][c] = jnp.where(hi == h, got, outs[k][c])
    return outs


def split_index(index):
    return index & (LANES - 1), index >> 7


def kernel(
    count,
    corr_count, fixed, positions_in, edges_in, rest_in, stiffness_in, corr_index_in,
    solution_out, residual_out,
    positions, edges, rest_length, stiffness, corr_index,
    index, rest, stiff, lo_hot, hi_hot, slope, terms,
    table, next_table, prev_table, pair_here, pair_prev, sums, search, product, search_product, twice,
    lower_sems, upper_sems, sum_sems, pair_sems, in_sems,
):
    me = lax.axis_index("gz")
    has_next = me < count - 1
    has_prev = me > 0
    upper = {"gz": jnp.minimum(me + 1, count - 1)}
    lower = {"gz": jnp.maximum(me - 1, 0)}
    parts = positions.shape[2] // LANES
    springs = rest_length.shape[1] // LANES
    slots = corr_index.shape[2] // LANES
    groups = springs // GROUP
    wide = GROUP * LANES
    f32, bf16 = jnp.float32, jnp.bfloat16

    loads = [
        pltpu.make_async_copy(source, place, in_sems.at[k])
        for k, (source, place) in enumerate((
            (corr_index_in, corr_index), (positions_in, positions), (edges_in, edges),
            (rest_in, rest_length), (stiffness_in, stiffness),
        ))
    ]
    for load in loads:
        load.start()
    barrier = pltpu.get_barrier_semaphore()
    for step in range(1, count):
        other = lax.rem(me + step, count)
        pl.semaphore_signal(barrier, inc=1, device_id={"gz": other}, device_id_type=MESH)

    def lanes(k):
        return slice(k * LANES, (k + 1) * LANES)

    for load in loads:
        load.wait()
    for s in range(slots):
        slot = s * LANES + lax.broadcasted_iota(jnp.int32, (1, LANES), 1)
        for c in range(2):
            pair_here[c, s : s + 1, :] = jnp.where(slot < corr_count[0], corr_index[0, c : c + 1, lanes(s)], -1)
    for c in range(2):
        for h in range(parts):
            table[0, c * parts + h : c * parts + h + 1, :] = positions[0, c : c + 1, lanes(h)]
    for k in range(springs):
        index[k : k + 1, :] = edges[0, 0:1, lanes(k)]
        index[springs + k : springs + k + 1, :] = edges[0, 1:2, lanes(k)]
        rest[k : k + 1, :] = rest_length[0:1, lanes(k)]
        stiff[k : k + 1, :] = stiffness[0:1, lanes(k)]

    @pl.when(me == 0)
    def _():
        pair_prev[...] = jnp.full_like(pair_prev, -1)
        prev_table[...] = jnp.zeros_like(prev_table)

    @pl.when(me == count - 1)
    def _():
        next_table[...] = jnp.zeros_like(next_table)

    search[...] = jnp.zeros_like(search)
    search_product[...] = jnp.zeros_like(search_product)
    twice[...] = jnp.zeros_like(twice)

    movable = (1 - fixed[0]).astype(f32)
    def lower_copy(turn):
        return pltpu.make_async_remote_copy(
            src_ref=table.at[turn], dst_ref=next_table.at[turn],
            send_sem=lower_sems.at[0, turn], recv_sem=lower_sems.at[1, turn],
            device_id=lower, device_id_type=MESH,
        )

    def upper_copy(turn):
        return pltpu.make_async_remote_copy(
            src_ref=table.at[turn], dst_ref=prev_table.at[turn],
            send_sem=upper_sems.at[0, turn], recv_sem=upper_sems.at[1, turn],
            device_id=upper, device_id_type=MESH,
        )

    pair_copy = pltpu.make_async_remote_copy(
        src_ref=pair_here, dst_ref=pair_prev,
        send_sem=pair_sems.at[0], recv_sem=pair_sems.at[1],
        device_id=upper, device_id_type=MESH,
    )

    def table_start(turn):
        @pl.when(has_prev)
        def _():
            lower_copy(turn).start()

        @pl.when(has_next)
        def _():
            upper_copy(turn).start()

    def table_wait(turn):
        @pl.when(has_next)
        def _():
            lower_copy(turn).wait_recv()

        @pl.when(has_prev)
        def _():
            upper_copy(turn).wait_recv()

    def sum_start(place, value):
        sums[place, me] = value
        for step in range(1, count):
            pltpu.make_async_remote_copy(
                src_ref=sums.at[place, me], dst_ref=sums.at[place, me],
                send_sem=sum_sems.at[0, place], recv_sem=sum_sems.at[1, place],
                device_id={"gz": lax.rem(me + step, count)}, device_id_type=MESH,
            ).start()

    def sum_all(place):
        part = sums.at[place, pl.ds(0, count - 1)]
        return pltpu.make_async_remote_copy(
            src_ref=part, dst_ref=part,
            send_sem=sum_sems.at[0, place], recv_sem=sum_sems.at[1, place],
            device_id={"gz": lax.rem(me + 1, count)}, device_id_type=MESH,
        )

    def sum_finish(place):
        sum_all(place).wait_recv()
        return jnp.sum(sums[place], axis=0)

    pl.semaphore_wait(barrier, count - 1)

    @pl.when(has_next)
    def _():
        pair_copy.start()

    table_start(0)

    def hot(line, chunk, sign):
        lo, hi = split_index(line)
        at = pl.ds(pl.multiple_of(chunk * LANES, LANES), LANES)
        rows = lax.broadcasted_iota(jnp.int32, (LANES, LANES), 0)
        lo_hot[:, at] = jnp.where(lo == rows, 1.0, 0.0).astype(bf16)
        rows = lax.broadcasted_iota(jnp.int32, (parts, LANES), 0)
        hi_hot[:, at] = jnp.where(hi == rows, sign, 0.0).astype(bf16)

    def hot_springs(k, _):
        hot(index[pl.ds(k, 1), :], k, 1.0)
        hot(index[pl.ds(springs + k, 1), :], springs + k, -1.0)
        return 0

    lax.fori_loop(0, springs, hot_springs, 0)
    for s in range(slots):
        hot(pair_here[0, s : s + 1, :], 2 * springs + s, 1.0)

    def rows_of(k):
        return pl.ds(pl.multiple_of(k * GROUP, GROUP), GROUP)

    def spread_of(turn, k):
        head = split_index(index[rows_of(k), :])
        tail = split_index(index[rows_of(k + groups), :])
        a, b = pick(lambda row: table[turn, row : row + 1, :], parts, [head, tail])
        return a[0] - b[0], a[1] - b[1]

    def corr_terms(turn):
        own = lambda row: table[turn, row : row + 1, :]
        near, before = pick(own, parts, [split_index(pair_here[0]), split_index(pair_prev[1])])
        (far,) = pick(lambda row: next_table[turn, row : row + 1, :], parts, [split_index(pair_here[1])])
        (behind,) = pick(lambda row: prev_table[turn, row : row + 1, :], parts, [split_index(pair_prev[0])])
        for c in range(2):
            put_terms(c, pl.ds(springs, slots), near[c] - far[c])
            put_terms(c, pl.ds(springs + slots, slots), behind[c] - before[c])

    def put_terms(c, rows, value):
        first = value.astype(bf16).astype(f32)
        terms[2 * c, rows, :] = first
        terms[2 * c + 1, rows, :] = value - first

    def spread_terms(row, lines):
        made = [[] for _ in lines]
        for i in range(GROUP):
            pieces = [[] for _ in lines]
            for part in range(4):
                value = jnp.broadcast_to(terms[part, pl.ds(row + i, 1), :], (parts, LANES)).astype(bf16)
                for piece, line in zip(pieces, lines):
                    at = pl.ds(pl.multiple_of((line + i) * LANES, LANES), LANES)
                    piece.append(value * hi_hot[:, at])
            for k, piece in enumerate(pieces):
                made[k].append(jnp.concatenate(piece, axis=0))
        return [jnp.concatenate(m, axis=1) for m in made]

    def add_terms(total, row, lines):
        for left, line in zip(spread_terms(row, lines), lines):
            right = lo_hot[:, pl.ds(pl.multiple_of(line * LANES, LANES), wide)]
            total += lax.dot_general(left, right, (((1,), (1,)), ((), ())), preferred_element_type=f32)
        return total

    def adjoint(turn, ready):
        def body(k, total):
            return add_terms(total, k * GROUP, (k * GROUP, springs + k * GROUP))

        total = lax.fori_loop(0, groups, body, jnp.zeros((4 * parts, LANES), f32), unroll=SCATTER_UNROLL)
        table_wait(turn)
        ready()
        corr_terms(turn)
        for s in range(0, 2 * slots, GROUP):
            total = add_terms(total, springs + s, (2 * springs + s,))
        return jnp.concatenate(
            [total[2 * c * parts : (2 * c + 1) * parts] + total[(2 * c + 1) * parts : (2 * c + 2) * parts]
             for c in range(2)], axis=0,
        )

    def first_springs(k, _):
        dx, dy = spread_of(0, k)
        rows = rows_of(k)
        length = jnp.sqrt((dx * dx + dy * dy) + 1.0)
        part = stiff[rows, :] * (length - rest[rows, :])
        for c, d in enumerate((dx, dy)):
            value = stiff[rows, :] * d / length
            slope[c, rows, :] = value
            put_terms(c, rows, value * part)
        return 0

    lax.fori_loop(0, groups, first_springs, 0, unroll=GATHER_UNROLL)

    def far_ready():
        @pl.when(has_prev)
        def _():
            pair_copy.wait_recv()

        for s in range(slots):
            hot(pair_prev[1, s : s + 1, :], 2 * springs + slots + s, -1.0)

    residual_out[...] = -movable * adjoint(0, far_ready)
    solution_out[...] = jnp.zeros_like(solution_out)

    def folded(value):
        return jnp.sum(value.reshape(-1, 8, LANES), axis=0)

    def matvec(turn, vector):
        def springs_body(k, _):
            dx, dy = spread_of(turn, k)
            rows = rows_of(k)
            part = slope[0, rows, :] * dx + slope[1, rows, :] * dy
            for c in range(2):
                put_terms(c, rows, slope[c, rows, :] * part)
            return 0

        lax.fori_loop(0, groups, springs_body, 0, unroll=GATHER_UNROLL)
        return movable * adjoint(turn, lambda: None) + DAMPING * vector[...]

    product[...] = residual_out[...]
    lane = lax.broadcasted_iota(jnp.int32, (1, LANES), 1)

    def turn_body(turn, before):
        norm_before, power_before = before
        if turn_copies(turn):
            table[turn] = movable * product[...]
            table_start(turn)

        residual = residual_out[...]
        dots = jnp.concatenate([
            jnp.sum(folded(residual * other), axis=0, keepdims=True)
            for other in (residual, product[...], search_product[...])
        ], axis=0)
        dots = jnp.sum(dots, axis=1, keepdims=True)
        sum_start(turn - 1, sum(jnp.where(lane == k, dots[k : k + 1], 0.0) for k in range(3)))
        image = matvec(turn, product) if turn_copies(turn) else None
        dots = sum_finish(turn - 1)
        norm, cross, mixed = (dots[:, k : k + 1] for k in range(3))
        live = turn > 1
        ratio = jnp.where(turn > 2, norm / norm_before, 0.0)
        power = cross + ratio * (2.0 * mixed + ratio * power_before)
        step_size = jnp.where(live, norm / power, 0.0)
        direction = residual_out[...] + ratio * search[...]
        moved = product[...] + ratio * search_product[...]
        search[...] = direction
        search_product[...] = moved
        solution_out[...] += step_size * direction
        residual_out[...] -= step_size * moved
        if image is not None:
            again = image + ratio * twice[...]
            twice[...] = again
            product[...] = jnp.where(live, product[...] - step_size * again, image)
        return norm, power

    def turn_copies(turn):
        return not isinstance(turn, int)

    ones = jnp.ones((1, 1), f32)
    last = lax.fori_loop(1, ITERS + 1, turn_body, (ones, ones))
    turn_body(ITERS + 1, last)

    @pl.when(has_next)
    def _():
        pair_copy.wait_send()
        for turn in range(ITERS + 1):
            upper_copy(turn).wait_send()

    @pl.when(has_prev)
    def _():
        for turn in range(ITERS + 1):
            lower_copy(turn).wait_send()

    for place in range(ITERS + 1):
        sum_all(place).wait_send()


def shards(count, positions, edges, rest_length, stiffness, corr_index, corr_count, fixed):
    verts, slots = positions.shape[2] // LANES, corr_index.shape[2] // LANES
    springs = rest_length.shape[1] // LANES
    columns = 2 * (springs + slots) * LANES
    turns = ITERS + 1
    f32 = jnp.float32
    out = jax.ShapeDtypeStruct((2 * verts, LANES), f32)
    vmem, smem = pl.BlockSpec(memory_space=pltpu.VMEM), pl.BlockSpec(memory_space=pltpu.SMEM)
    answer, residual = pl.pallas_call(
        functools.partial(kernel, count),
        out_shape=(out, out),
        in_specs=[smem, smem] + [pl.BlockSpec(memory_space=pltpu.HBM)] * 5,
        out_specs=(vmem, vmem),
        scratch_shapes=[
            pltpu.VMEM(positions.shape, f32),
            pltpu.VMEM(edges.shape, jnp.int32),
            pltpu.VMEM(rest_length.shape, f32),
            pltpu.VMEM(stiffness.shape, f32),
            pltpu.VMEM(corr_index.shape, jnp.int32),
            pltpu.VMEM((2 * springs, LANES), jnp.int32),
            pltpu.VMEM((springs, LANES), f32),
            pltpu.VMEM((springs, LANES), f32),
            pltpu.VMEM((LANES, columns), jnp.bfloat16),
            pltpu.VMEM((verts, columns), jnp.bfloat16),
            pltpu.VMEM((2, springs, LANES), f32),
            pltpu.VMEM((4, springs + 2 * slots, LANES), f32),
            pltpu.VMEM((turns, 2 * verts, LANES), f32),
            pltpu.VMEM((turns, 2 * verts, LANES), f32),
            pltpu.VMEM((turns, 2 * verts, LANES), f32),
            pltpu.VMEM((2, slots, LANES), jnp.int32),
            pltpu.VMEM((2, slots, LANES), jnp.int32),
            pltpu.VMEM((turns, count, 1, LANES), f32),
            pltpu.VMEM((2 * verts, LANES), f32),
            pltpu.VMEM((2 * verts, LANES), f32),
            pltpu.VMEM((2 * verts, LANES), f32),
            pltpu.VMEM((2 * verts, LANES), f32),
            pltpu.SemaphoreType.DMA((2, turns)),
            pltpu.SemaphoreType.DMA((2, turns)),
            pltpu.SemaphoreType.DMA((2, turns)),
            pltpu.SemaphoreType.DMA((2,)),
            pltpu.SemaphoreType.DMA((5,)),
        ],
        compiler_params=pltpu.CompilerParams(
            collective_id=0, has_side_effects=True, vmem_limit_bytes=40 * 2**20
        ),
        name="align",
    )(corr_count, fixed, positions, edges, rest_length, stiffness, corr_index)
    return answer.reshape(positions.shape), residual.reshape(positions.shape)


def solution(mesh):
    row = P(("groups", "gz"))
    return jax.shard_map(
        functools.partial(shards, mesh.shape["gz"]),
        mesh=mesh,
        in_specs=(row,) * 7,
        out_specs=(row, row),
        check_vma=False,
    )
```

time: 53.3 us -> 40.6 us (0.76)
  Pallas kernels: 45.9 us -> 33.1 us
    pallas_call x1, Pallas kernels: 45.9 us -> 33.1 us  [shards(): pl.pallas_call(functools.partial(kernel, count), out_shape=(out, out), in...]
where the time goes in v2:
time: 40.6 us; the launch traced here: 40.2 us
  Pallas kernels  33.1 us (82%)
  local copies, waits for them, and re-layouts  5.07 us (12%)
  between operations  1.94 us (5%)
    pallas_call x1, Pallas kernels, shards(): pl.pallas_call(functools.partial(kernel, count), out_shape=(out, out), in...  33.1 us
    unnamed x10, local copies, waits for them, and re-layouts  3.8 us
    reshape x2, local copies, waits for them, and re-layouts, shards(): return (answer.reshape(positions.shape), residual.reshape(positions.shape))  1.27 us

profile of v2, /device:TPU:0, one launch (start us, length us, event | category | flops | bytes accessed | tf_op | source)
XLA Modules:
  0.0 40.2 jit_solution(17380163467023911342)
XLA Ops:
  1.9 0.0 copy-start
  1.9 0.8 %copy-done = s32[1,2,8192]{2,1,0:T(2,128)S(1)} copy-done((s32[1,2,8192]{2,1,0:T(2,128)S(1)}, s32[1,2,8192]{2,1,0:T(2,128)}, u32[]{:S(2)}) %copy-start) | copy-done | bytes 65560
  2.8 0.0 copy-start.1
  2.8 0.8 %copy-done.1 = f32[1,2,4096]{2,1,0:T(2,128)S(1)} copy-done((f32[1,2,4096]{2,1,0:T(2,128)S(1)}, f32[1,2,4096]{2,1,0:T(2,128)}, u32[]{:S(2)}) %copy-start.1) | copy-done | bytes 32792
  3.5 0.0 copy-start.2
  3.5 0.8 %copy-done.2 = f32[1,8192]{1,0:T(1,128)S(1)} copy-done((f32[1,8192]{1,0:T(1,128)S(1)}, f32[1,8192]{1,0:T(1,128)}, u32[]{:S(2)}) %copy-start.2) | copy-done | bytes 32792
  4.3 0.0 copy-start.3
  4.3 0.8 %copy-done.3 = f32[1,8192]{1,0:T(1,128)S(1)} copy-done((f32[1,8192]{1,0:T(1,128)S(1)}, f32[1,8192]{1,0:T(1,128)}, u32[]{:S(2)}) %copy-start.3) | copy-done | bytes 32792
  5.0 0.0 copy-start.4
  5.0 0.7 %copy-done.4 = s32[1,2,1024]{2,1,0:T(2,128)S(1)} copy-done((s32[1,2,1024]{2,1,0:T(2,128)S(1)}, s32[1,2,1024]{2,1,0:T(2,128)}, u32[]{:S(2)}) %copy-start.4) | copy-done | bytes 8216
  5.7 33.1 %align.1 = (f32[64,128]{1,0:T(8,128)S(1)}, f32[64,128]{1,0:T(8,128)S(1)}) custom-call(s32[1]{0:T(128)S(6)} %copy.9.corr_count, s32[1]{0:T(128)S(6)} %copy.10.fixed, f32[1,2,4096]{2,1,0:T(2,128)S(1)} %copy-done.1, s32[1,2,8192]{2,1,0:T(2,128)S(1)} %copy-done, f32[1,8192]{1,0:T(1,128)S(1)} %copy-done.2, f32[1,8192]{1,0:T(1,128)S(1)} %copy-done.3, ...), custom_call_target="tpu_custom_call" | custom-call | tf_op jit(solution)/shard_map/align/pallas_call | solution.py:348
  38.9 0.6 %reshape.10 = f32[1,2,4096]{2,1,0:T(2,128)} reshape(f32[64,128]{1,0:T(8,128)S(1)} %get-tuple-element.4) | data formatting | bytes 65536 | tf_op jit(solution)/shard_map/reshape | solution.py:387
  39.5 0.6 %reshape.11 = f32[1,2,4096]{2,1,0:T(2,128)} reshape(f32[64,128]{1,0:T(8,128)S(1)} %get-tuple-element.5) | data formatting | bytes 65536 | tf_op jit(solution)/shard_map/reshape | solution.py:387
Async XLA Ops:
  1.9 0.8 %copy-start = (s32[1,2,8192]{2,1,0:T(2,128)S(1)}, s32[1,2,8192]{2,1,0:T(2,128)}, u32[]{:S(2)}) copy-start(s32[1,2,8192]{2,1,0:T(2,128)} %edges_in.1) | copy-start | bytes 196612
  2.8 0.8 %copy-start.1 = (f32[1,2,4096]{2,1,0:T(2,128)S(1)}, f32[1,2,4096]{2,1,0:T(2,128)}, u32[]{:S(2)}) copy-start(f32[1,2,4096]{2,1,0:T(2,128)} %positions_in.1) | copy-start | bytes 98308
  3.5 0.8 %copy-start.2 = (f32[1,8192]{1,0:T(1,128)S(1)}, f32[1,8192]{1,0:T(1,128)}, u32[]{:S(2)}) copy-start(f32[1,8192]{1,0:T(1,128)} %rest_in.1) | copy-start | bytes 98308
  4.3 0.8 %copy-start.3 = (f32[1,8192]{1,0:T(1,128)S(1)}, f32[1,8192]{1,0:T(1,128)}, u32[]{:S(2)}) copy-start(f32[1,8192]{1,0:T(1,128)} %stiffness_in.1) | copy-start | bytes 98308
  5.0 0.7 %copy-start.4 = (s32[1,2,1024]{2,1,0:T(2,128)S(1)}, s32[1,2,1024]{2,1,0:T(2,128)}, u32[]{:S(2)}) copy-start(s32[1,2,1024]{2,1,0:T(2,128)} %corr_index_in.1) | copy-start | bytes 24580

commit v3 on v2

--- a/solution.py
+++ b/solution.py
@@ -11,6 +11,7 @@
 DAMPING = 0.05
 LANES = 128
 GROUP = 8
+SPLITS = 3
 GATHER_UNROLL = 8
 SCATTER_UNROLL = 8
 MESH = pl.DeviceIdType.MESH
@@ -39,7 +40,7 @@
     solution_out, residual_out,
     positions, edges, rest_length, stiffness, corr_index,
     index, rest, stiff, lo_hot, hi_hot, slope, terms,
-    table, next_table, prev_table, pair_here, pair_prev, sums, search, product, search_product, twice,
+    table, next_table, prev_table, pair_here, pair_prev, sums, sums_now, search, product, search_product, twice,
     lower_sems, upper_sems, sum_sems, pair_sems, in_sems,
 ):
     me = lax.axis_index("gz")
@@ -203,15 +204,16 @@
             put_terms(c, pl.ds(springs + slots, slots), behind[c] - before[c])
 
     def put_terms(c, rows, value):
-        first = value.astype(bf16).astype(f32)
-        terms[2 * c, rows, :] = first
-        terms[2 * c + 1, rows, :] = value - first
+        for k in range(SPLITS):
+            piece = value if k == SPLITS - 1 else value.astype(bf16).astype(f32)
+            terms[SPLITS * c + k, rows, :] = piece
+            value = value - piece
 
     def spread_terms(row, lines):
         made = [[] for _ in lines]
         for i in range(GROUP):
             pieces = [[] for _ in lines]
-            for part in range(4):
+            for part in range(2 * SPLITS):
                 value = jnp.broadcast_to(terms[part, pl.ds(row + i, 1), :], (parts, LANES)).astype(bf16)
                 for piece, line in zip(pieces, lines):
                     at = pl.ds(pl.multiple_of((line + i) * LANES, LANES), LANES)
@@ -230,16 +232,14 @@
         def body(k, total):
             return add_terms(total, k * GROUP, (k * GROUP, springs + k * GROUP))
 
-        total = lax.fori_loop(0, groups, body, jnp.zeros((4 * parts, LANES), f32), unroll=SCATTER_UNROLL)
+        total = lax.fori_loop(0, groups, body, jnp.zeros((2 * SPLITS * parts, LANES), f32), unroll=SCATTER_UNROLL)
         table_wait(turn)
         ready()
         corr_terms(turn)
         for s in range(0, 2 * slots, GROUP):
             total = add_terms(total, springs + s, (2 * springs + s,))
-        return jnp.concatenate(
-            [total[2 * c * parts : (2 * c + 1) * parts] + total[(2 * c + 1) * parts : (2 * c + 2) * parts]
-             for c in range(2)], axis=0,
-        )
+        total = total.reshape(2, SPLITS, parts, LANES)
+        return jnp.concatenate([sum(total[c, k] for k in range(SPLITS)) for c in range(2)], axis=0)
 
     def first_springs(k, _):
         dx, dy = spread_of(0, k)
@@ -281,23 +281,33 @@
         return movable * adjoint(turn, lambda: None) + DAMPING * vector[...]
 
     product[...] = residual_out[...]
+    sums_now[...] = jnp.zeros_like(sums_now)
     lane = lax.broadcasted_iota(jnp.int32, (1, LANES), 1)
 
     def turn_body(turn, before):
         norm_before, power_before = before
-        if turn_copies(turn):
-            table[turn] = movable * product[...]
-            table_start(turn)
-
         residual = residual_out[...]
         dots = jnp.concatenate([
             jnp.sum(folded(residual * other), axis=0, keepdims=True)
             for other in (residual, product[...], search_product[...])
         ], axis=0)
         dots = jnp.sum(dots, axis=1, keepdims=True)
-        sum_start(turn - 1, sum(jnp.where(lane == k, dots[k : k + 1], 0.0) for k in range(3)))
+        row = sum(jnp.where(lane == k, dots[k : k + 1], 0.0) for k in range(3))
+
+        @pl.when(turn > 1)
+        def _():
+            sum_start(turn - 2, row)
+
+        if turn_copies(turn):
+            table[turn] = movable * product[...]
+            table_start(turn)
         image = matvec(turn, product) if turn_copies(turn) else None
-        dots = sum_finish(turn - 1)
+
+        @pl.when(turn > 1)
+        def _():
+            sums_now[...] = sum_finish(turn - 2)
+
+        dots = sums_now[...]
         norm, cross, mixed = (dots[:, k : k + 1] for k in range(3))
         live = turn > 1
         ratio = jnp.where(turn > 2, norm / norm_before, 0.0)
@@ -333,7 +343,7 @@
         for turn in range(ITERS + 1):
             lower_copy(turn).wait_send()
 
-    for place in range(ITERS + 1):
+    for place in range(ITERS):
         sum_all(place).wait_send()
 
 
@@ -362,13 +372,14 @@
             pltpu.VMEM((LANES, columns), jnp.bfloat16),
             pltpu.VMEM((verts, columns), jnp.bfloat16),
             pltpu.VMEM((2, springs, LANES), f32),
-            pltpu.VMEM((4, springs + 2 * slots, LANES), f32),
+            pltpu.VMEM((2 * SPLITS, springs + 2 * slots, LANES), f32),
             pltpu.VMEM((turns, 2 * verts, LANES), f32),
             pltpu.VMEM((turns, 2 * verts, LANES), f32),
             pltpu.VMEM((turns, 2 * verts, LANES), f32),
             pltpu.VMEM((2, slots, LANES), jnp.int32),
             pltpu.VMEM((2, slots, LANES), jnp.int32),
-            pltpu.VMEM((turns, count, 1, LANES), f32),
+            pltpu.VMEM((ITERS, count, 1, LANES), f32),
+            pltpu.VMEM((1, LANES), f32),
             pltpu.VMEM((2 * verts, LANES), f32),
             pltpu.VMEM((2 * verts, LANES), f32),
             pltpu.VMEM((2 * verts, LANES), f32),

time: 40.6 us -> 41.2 us (1.015)
  Pallas kernels: 33.1 us -> 33.7 us
    pallas_call x1, Pallas kernels: 33.1 us -> 33.7 us  [shards(): pl.pallas_call(functools.partial(kernel, count), out_shape=(out, out), in...]
where the time goes in v3:
time: 41.2 us; the launch traced here: 40.8 us
  Pallas kernels  33.7 us (82%)
  local copies, waits for them, and re-layouts  5.07 us (12%)
  between operations  1.94 us (5%)
    pallas_call x1, Pallas kernels, shards(): pl.pallas_call(functools.partial(kernel, count), out_shape=(out, out), in...  33.7 us
    unnamed x10, local copies, waits for them, and re-layouts  3.8 us
    reshape x2, local copies, waits for them, and re-layouts, shards(): return (answer.reshape(positions.shape), residual.reshape(positions.shape))  1.27 us

profile of v3, /device:TPU:0, one launch (start us, length us, event | category | flops | bytes accessed | tf_op | source)
XLA Modules:
  0.0 40.8 jit_solution(9761957387983649223)
XLA Ops:
  1.9 0.0 copy-start
  1.9 0.8 %copy-done = s32[1,2,8192]{2,1,0:T(2,128)S(1)} copy-done((s32[1,2,8192]{2,1,0:T(2,128)S(1)}, s32[1,2,8192]{2,1,0:T(2,128)}, u32[]{:S(2)}) %copy-start) | copy-done | bytes 65560
  2.8 0.0 copy-start.1
  2.8 0.8 %copy-done.1 = f32[1,2,4096]{2,1,0:T(2,128)S(1)} copy-done((f32[1,2,4096]{2,1,0:T(2,128)S(1)}, f32[1,2,4096]{2,1,0:T(2,128)}, u32[]{:S(2)}) %copy-start.1) | copy-done | bytes 32792
  3.5 0.0 copy-start.2
  3.5 0.8 %copy-done.2 = f32[1,8192]{1,0:T(1,128)S(1)} copy-done((f32[1,8192]{1,0:T(1,128)S(1)}, f32[1,8192]{1,0:T(1,128)}, u32[]{:S(2)}) %copy-start.2) | copy-done | bytes 32792
  4.3 0.0 copy-start.3
  4.3 0.8 %copy-done.3 = f32[1,8192]{1,0:T(1,128)S(1)} copy-done((f32[1,8192]{1,0:T(1,128)S(1)}, f32[1,8192]{1,0:T(1,128)}, u32[]{:S(2)}) %copy-start.3) | copy-done | bytes 32792
  5.0 0.0 copy-start.4
  5.0 0.7 %copy-done.4 = s32[1,2,1024]{2,1,0:T(2,128)S(1)} copy-done((s32[1,2,1024]{2,1,0:T(2,128)S(1)}, s32[1,2,1024]{2,1,0:T(2,128)}, u32[]{:S(2)}) %copy-start.4) | copy-done | bytes 8216
  5.7 33.7 %align.1 = (f32[64,128]{1,0:T(8,128)S(1)}, f32[64,128]{1,0:T(8,128)S(1)}) custom-call(s32[1]{0:T(128)S(6)} %copy.9.corr_count, s32[1]{0:T(128)S(6)} %copy.10.fixed, f32[1,2,4096]{2,1,0:T(2,128)S(1)} %copy-done.1, s32[1,2,8192]{2,1,0:T(2,128)S(1)} %copy-done, f32[1,8192]{1,0:T(1,128)S(1)} %copy-done.2, f32[1,8192]{1,0:T(1,128)S(1)} %copy-done.3, ...), custom_call_target="tpu_custom_call" | custom-call | tf_op jit(solution)/shard_map/align/pallas_call | solution.py:358
  39.5 0.6 %reshape.10 = f32[1,2,4096]{2,1,0:T(2,128)} reshape(f32[64,128]{1,0:T(8,128)S(1)} %get-tuple-element.4) | data formatting | bytes 65536 | tf_op jit(solution)/shard_map/reshape | solution.py:398
  40.1 0.6 %reshape.11 = f32[1,2,4096]{2,1,0:T(2,128)} reshape(f32[64,128]{1,0:T(8,128)S(1)} %get-tuple-element.5) | data formatting | bytes 65536 | tf_op jit(solution)/shard_map/reshape | solution.py:398
Async XLA Ops:
  1.9 0.8 %copy-start = (s32[1,2,8192]{2,1,0:T(2,128)S(1)}, s32[1,2,8192]{2,1,0:T(2,128)}, u32[]{:S(2)}) copy-start(s32[1,2,8192]{2,1,0:T(2,128)} %edges_in.1) | copy-start | bytes 196612
  2.8 0.8 %copy-start.1 = (f32[1,2,4096]{2,1,0:T(2,128)S(1)}, f32[1,2,4096]{2,1,0:T(2,128)}, u32[]{:S(2)}) copy-start(f32[1,2,4096]{2,1,0:T(2,128)} %positions_in.1) | copy-start | bytes 98308
  3.5 0.8 %copy-start.2 = (f32[1,8192]{1,0:T(1,128)S(1)}, f32[1,8192]{1,0:T(1,128)}, u32[]{:S(2)}) copy-start(f32[1,8192]{1,0:T(1,128)} %rest_in.1) | copy-start | bytes 98308
  4.3 0.8 %copy-start.3 = (f32[1,8192]{1,0:T(1,128)S(1)}, f32[1,8192]{1,0:T(1,128)}, u32[]{:S(2)}) copy-start(f32[1,8192]{1,0:T(1,128)} %stiffness_in.1) | copy-start | bytes 98308
  5.0 0.7 %copy-start.4 = (s32[1,2,1024]{2,1,0:T(2,128)S(1)}, s32[1,2,1024]{2,1,0:T(2,128)}, u32[]{:S(2)}) copy-start(s32[1,2,1024]{2,1,0:T(2,128)} %corr_index_in.1) | copy-start | bytes 24580
